TPU v7x, 32 devices: a whole 2x2x4 slice. The times are simulated.
32 devices in a mesh: inl: 8 (over z, y), off: 4 (over x, core).
Axes of the slice: x: 2, y: 2, z: 4, core: 2. Of those that a mesh axis runs over, the one named last changes fastest.
Arguments:
- traces: bfloat16 [4, 4096, 4096], P('off', 'inl'), may hold values from -24 to 24, as said below
- owner: int32 [4, 4096, 1], P('off', 'inl'), may hold values from 0 to 7; in each aligned block of 512 rows (0 to 511, 512 to 1023, ..., all dimensions but the last counted through in order) at most 192 rows name the same one
- local_bin: int32 [4, 4096], P('off', 'inl'), may hold values from 0 to 63
- live_count: int32 [4, 8], P('off', 'inl'), may hold values from 256 to 512, as said below
- xl_gain: float32 [16], replicated, may hold values from 0.2 to 1
- il_gain: float32 [32], replicated, may hold values from 0.2 to 1
Outputs:
- volume: bfloat16 [4, 16, 32, 4096], P('off', 'inl')
Inputs may be any that keep to these rules, and one draw needn't show every extreme that they name: `traces`: every trace amplitude lies in this range. Among the traces of one device no owner is named more than 192 times; some device names one owner exactly 192 times. The first live_count traces of a device are live; some device has all 512 traces live.
All inputs are finite; a program needn't handle non-finite values.
Results may differ from a plain program's by a relative error of at most 0.024.
Values may be sent and summed in bfloat16 or wider, within the bound.
A program may use at most 128 MiB of HBM per device.

v0:
```python
import math
import jax
import jax.numpy as jnp
from jax import lax
from jax.sharding import PartitionSpec as P

NLAG = 80
damping = 0.1


def levinson(series):
    order = series.shape[0]
    error = series[0] + damping
    coeffs = jnp.zeros_like(series).at[0].set(1.0)
    for section in range(1, order):
        partial_sum = jnp.sum(coeffs[:section] * series[section:0:-1], axis=0)
        reflection = -partial_sum / error
        update = coeffs[: section + 1] + reflection * coeffs[section::-1]
        coeffs = coeffs.at[: section + 1].set(update)
        error = error * (1.0 - reflection * reflection)
    return coeffs


def smooth_matrix(gain, reach):
    width = gain.shape[0]
    index = jnp.arange(width)
    distance = jnp.abs(index[:, None] - index[None, :])
    weight = jnp.take(gain, distance) * jnp.exp(-distance.astype(gain.dtype) / reach)
    return (weight / jnp.sum(weight, axis=1, keepdims=True)).astype(jnp.bfloat16)


def autocorrelate(block_rows):
    number, samples = block_rows.shape
    groups = samples // 128

    def autocorrelate_one_block(part_rows):
        height = part_rows.shape[0]
        leading = part_rows.reshape(height, groups, 128)
        following = jnp.pad(part_rows[:, 128:], ((0, 0), (0, 128))).reshape(height, groups, 128)
        within = jnp.einsum("nab,nac->nbc", leading, leading, preferred_element_type=jnp.float32)
        across = jnp.einsum("nab,nac->nbc", leading, following, preferred_element_type=jnp.float32)
        total = within[:, 0, :]
        for offset in range(1, 128):
            total = total + jnp.concatenate(
                [within[:, offset, offset:], across[:, offset, :offset]], axis=1
            )
        return total

    block = math.gcd(number, 64)
    result = lax.map(autocorrelate_one_block, block_rows.reshape(number // block, block, samples))
    return result.reshape(number, 128)


def apply_filter(stacked, filters):
    number, samples = stacked.shape
    taps = filters.shape[1]
    groups = samples // 128
    column = jnp.arange(256)[None, :, None]
    output_pos = jnp.arange(128)[None, None, :]
    lag_index = jnp.arange(taps)[:, None, None]
    table = (column == output_pos + 128 - lag_index).astype(jnp.bfloat16)

    def apply_one_block(pair):
        part_rows, part_filters = pair
        height = part_rows.shape[0]
        kernel = jnp.einsum(
            "nj,jcb->ncb", part_filters, table, preferred_element_type=jnp.float32
        ).astype(jnp.bfloat16)
        padded = jnp.pad(part_rows, ((0, 0), (128, 0))).reshape(height, groups + 1, 128)
        windows = jnp.concatenate([padded[:, :-1], padded[:, 1:]], axis=2)
        result = jnp.einsum("nac,ncb->nab", windows, kernel, preferred_element_type=jnp.float32)
        return result.reshape(height, samples).astype(jnp.bfloat16)

    block = math.gcd(number, 64)
    result = lax.map(
        apply_one_block,
        (
            stacked.reshape(number // block, block, samples),
            filters.reshape(number // block, block, taps),
        ),
    )
    return result.reshape(number, samples)


def shards(traces, owner, local_bin, live_count, xl_gain, il_gain):
    devices = lax.axis_size("inl")
    traces_here = traces.shape[1]
    samples = traces.shape[2]
    shot_rows = traces[0]
    slots = max(2, 3 * traces_here // devices)
    crosslines = xl_gain.shape[0]
    inlines = il_gain.shape[0]
    inline_dev = inlines // devices
    bins_here = inline_dev * crosslines
    destination = owner[0, :, 0]
    alive = jnp.arange(traces_here, dtype=jnp.int32) < live_count[0, 0]
    target = jnp.where(alive, local_bin[0], -1)
    matches = (destination[:, None] == jnp.arange(devices, dtype=jnp.int32)[None, :]).astype(
        jnp.int32
    )
    places = jnp.sum((jnp.cumsum(matches, axis=0) - matches) * matches, axis=1)
    position = destination * slots + places
    source_slot = (
        jnp.full((devices * slots,), traces_here, jnp.int32)
        .at[position]
        .set(jnp.arange(traces_here, dtype=jnp.int32))
    )
    send_bins = jnp.take(target, source_slot, axis=0, mode="fill", fill_value=-1)
    send_rows = jnp.take(shot_rows, source_slot, axis=0, mode="fill", fill_value=0)
    arrived, arrived_bins = (
        lax.all_to_all(
            send_rows.reshape(devices, slots, samples),
            "inl",
            split_axis=0,
            concat_axis=0,
            tiled=True,
        ),
        lax.all_to_all(
            send_bins.reshape(devices, slots), "inl", split_axis=0, concat_axis=0, tiled=True
        ),
    )
    arrived = arrived.reshape(devices * slots, samples)
    arrived_lags = autocorrelate(arrived)
    arrived_bins = arrived_bins.reshape(devices * slots)
    onehot = arrived_bins[:, None] == jnp.arange(bins_here, dtype=jnp.int32)[None, :]
    counts = jnp.sum(onehot.astype(jnp.float32), axis=0)
    contract = (((0,), (0,)), ((), ()))
    stack_sum = lax.dot_general(
        onehot.astype(jnp.bfloat16), arrived, contract, preferred_element_type=jnp.float32
    )
    lag_sum = lax.dot_general(
        onehot.astype(jnp.float32),
        arrived_lags[:, :NLAG],
        contract,
        precision=lax.Precision.HIGHEST,
        preferred_element_type=jnp.float32,
    )
    lag_total = lax.psum(lag_sum.astype(jnp.bfloat16), "off").astype(jnp.float32)
    stacked = (stack_sum / jnp.maximum(counts, 1.0)[:, None]).astype(jnp.bfloat16)
    rho = lag_total / jnp.maximum(lag_total[:, :1], 1.0)
    filters = levinson(rho.T).T.astype(jnp.bfloat16)
    decon = apply_filter(stacked, filters)
    cross_matrix = smooth_matrix(xl_gain, crosslines / 16.0)
    smoothed = jnp.einsum(
        "xy,iyt->ixt",
        cross_matrix,
        decon.reshape(inline_dev, crosslines, samples),
        preferred_element_type=jnp.float32,
    ).astype(jnp.bfloat16)
    relaid = lax.all_to_all(smoothed, "inl", split_axis=1, concat_axis=0, tiled=True)
    inline_matrix = smooth_matrix(il_gain, 2.0 * inline_dev)
    result = jnp.einsum(
        "ij,jxt->xit", inline_matrix, relaid, preferred_element_type=jnp.float32
    ).astype(jnp.bfloat16)
    return result[None]


def solution(mesh):
    placed = (
        P("off", "inl", None),
        P("off", "inl", None),
        P("off", "inl"),
        P("off", "inl"),
        P(),
        P(),
    )
    return jax.shard_map(
        shards, mesh=mesh, in_specs=placed, out_specs=P("off", "inl", None, None), check_vma=False
    )
```

profile of v0, /device:TPU:0, one launch (start us, length us, event | category | flops | bytes accessed | tf_op | source)
XLA Modules:
  0.0 1120.3 jit_solution(14159218616566697119)
XLA Ops:
  3.6 2.4 scatter_custom_fusion
  7.4 9.5 gather_fusion
  17.5 7.3 all-to-all-start
  24.9 24.8 %gather_fusion.1 = bf16[1536,4096]{1,0:T(8,128)(2,1)} fusion(bf16[512,4096]{1,0:T(8,128)(2,1)} %bitcast.1481, s32[2048]{0:T(1024)S(1)} %pad_clamp_fusion), kind=kCustom, calls=%fused_computation.1 | custom fusion | bytes 25171968 | tf_op jit(solution)/shard_map/jit(_take)/gather | solution.py:109
  49.7 10.7 broadcast_select_fusion
  60.3 6.1 all-to-all-start.1
  66.6 1.9 gather_fusion.2
  68.9 270.0 %all-to-all-done.1 = bf16[8,192,4096]{2,1,0:T(8,128)(2,1)} async-done(((bf16[8,192,4096]{2,1,0:T(8,128)(2,1)}), bf16[8,192,4096]{2,1,0:T(8,128)(2,1)}, u32[]{:S(2)}, u32[]{:S(2)}) %all-to-all-start.1) | async-done | bytes 12582944 | tf_op jit(solution)/shard_map/all_to_all | solution.py:111
  339.0 706.3 %while.97 = (s32[]{:T(128)}, f32[24,64,128]{2,1,0:T(8,128)S(1)}, bf16[24,64,4096]{2,1,0:T(8,128)(2,1)}, s32[]{:T(128)}) while((s32[]{:T(128)}, f32[24,64,128]{2,1,0:T(8,128)S(1)}, bf16[24,64,4096]{2,1,0:T(8,128)(2,1)}, s32[]{:T(128)}) %tuple.473), condition=%wide.region_6.7_spmd, body=%wide.region_5.6_spmd.sunk | while | flops 136298496 | bytes 32456764 | solution.py:50
  339.1 1.2 dynamic-slice_bitcast_fusion.3
  365.8 2.3 fusion.197
  368.2 1.2 dynamic-slice_bitcast_fusion.3
  394.9 2.3 fusion.197
  397.2 1.2 dynamic-slice_bitcast_fusion.3
  423.9 2.3 fusion.197
  426.3 1.2 dynamic-slice_bitcast_fusion.3
  453.0 2.3 fusion.197
  482.0 2.3 fusion.197
  484.3 1.2 dynamic-slice_bitcast_fusion.3
  511.1 2.3 fusion.197
  540.1 2.3 fusion.197
  569.1 2.3 fusion.197
  598.2 2.3 fusion.197
  627.2 2.3 fusion.197
  656.3 2.3 fusion.197
  685.3 2.3 fusion.197
  714.4 2.3 fusion.197
  743.4 2.3 fusion.197
  745.7 1.2 dynamic-slice_bitcast_fusion.3
  772.5 2.3 fusion.197
  801.5 2.3 fusion.197
  803.8 1.2 dynamic-slice_bitcast_fusion.3
  830.5 2.3 fusion.197
  859.6 2.3 fusion.197
  888.6 2.3 fusion.197
  917.7 2.3 fusion.197
  946.7 2.3 fusion.197
  975.8 2.3 fusion.197
  1004.8 2.3 fusion.197
  1033.8 2.3 fusion.197
  1046.0 10.3 psum.7
  1083.9 6.9 fusion.124
  1091.5 2.7 fusion.129
  1094.1 4.1 fusion.130
  1098.8 1.2 copy.1305
  1100.0 4.7 all-to-all-start.2
  1104.8 6.6 gather_fusion.3
  1111.5 7.0 all-to-all-done.2
  (6863 shorter events, 617.9 us)
Async XLA Ops:
  0.0 1104.8 %copy-start = (f32[32]{0:T(128)S(1)}, f32[32]{0:T(128)}, u32[]{:S(2)}) copy-start(f32[32]{0:T(128)} %param.175) | copy-start | bytes 388
  17.5 42.8 %all-to-all-start = ((s32[8,1,192]{2,1,0:T(1,128)}), s32[8,1,192]{2,1,0:T(1,128)S(1)}, u32[]{:S(2)}, u32[]{:S(2)}) async-start(s32[8,1,192]{2,1,0:T(1,128)} %select_n.89), calls=%async_computation | async-start | bytes 16384 | tf_op jit(solution)/shard_map/all_to_all | solution.py:118
  60.3 6.2 copy-start.1
  60.3 278.6 %all-to-all-start.1 = ((bf16[8,192,4096]{2,1,0:T(8,128)(2,1)}), bf16[8,192,4096]{2,1,0:T(8,128)(2,1)}, u32[]{:S(2)}, u32[]{:S(2)}) async-start(bf16[8,192,4096]{2,1,0:T(8,128)(2,1)} %broadcast_select_fusion), calls=%async_computation.1 | async-start | bytes 25165824 | tf_op jit(solution)/shard_map/all_to_all | solution.py:111
  338.9 718.5 %copy-start.2 = (f32[80,64]{1,0:T(8,128)S(1)}, f32[80,64]{1,0:T(8,128)}, u32[]{:S(2)}) copy-start(f32[80,64]{1,0:T(8,128)} %constant.1976.clone.1) | copy-start | bytes 61444
  338.9 718.5 %copy-start.3 = (f32[2,64]{1,0:T(2,128)S(1)}, f32[2,64]{1,0:T(2,128)}, u32[]{:S(2)}) copy-start(f32[2,64]{1,0:T(2,128)} %constant.1978.clone.1) | copy-start | bytes 1540
  338.9 718.5 %copy-start.4 = (f32[2,64]{1,0:T(2,128)S(1)}, f32[2,64]{1,0:T(2,128)}, u32[]{:S(2)}) copy-start(f32[2,64]{1,0:T(2,128)} %constant.1979.clone.1) | copy-start | bytes 1540
  1100.0 18.5 %all-to-all-start.2 = ((bf16[4,16,4096]{2,0,1:T(4,128)(2,1)}), bf16[4,16,4096]{2,0,1:T(4,128)(2,1)S(1)}, u32[]{:S(2)}, u32[]{:S(2)}) async-start(bf16[4,16,4096]{2,0,1:T(4,128)(2,1)} %copy.1305), calls=%async_computation.2 | async-start | bytes 1048576 | tf_op jit(solution)/shard_map/all_to_all | solution.py:150
where the time goes:
time: 1130 us; the launch traced here: 1120 us
  local copies, waits for them, and re-layouts  626 us (55%)
  waiting for transfers between devices  277 us (25%)
  other arithmetic  73.6 us (7%)
  loops' own time  59.2 us (5%)
  matrix products  52.5 us (5%)
  starting transfers between devices  18.1 us (2%)
    slice x3048, local copies, waits for them, and re-layouts, autocorrelate_one_block(): within[:, offset, offset:]  406 us
    all_to_all x1, waiting for transfers between devices, shards(): lax.all_to_all(send_rows.reshape(devices, slots, samples), 'inl', split_a...  270 us
    slice x3048, local copies, waits for them, and re-layouts, autocorrelate_one_block(): across[:, offset, :offset]  113 us
    another operation x1, loops' own time, autocorrelate(): lax.map(autocorrelate_one_block, block_rows.reshape(number // block, bloc...  59.2 us
    dynamic_update_slice x24, other arithmetic, autocorrelate(): lax.map(autocorrelate_one_block, block_rows.reshape(number // block, bloc...  55.5 us
    squeeze x24, local copies, waits for them, and re-layouts, autocorrelate(): lax.map(autocorrelate_one_block, block_rows.reshape(number // block, bloc...  28.3 us
    gather x1, local copies, waits for them, and re-layouts, shards(): jnp.take(shot_rows, source_slot, axis=0, mode='fill', fill_value=0)  24.8 us

commit v1 on v0

--- a/solution.py
+++ b/solution.py
@@ -1,11 +1,46 @@
+import functools
 import math
 import jax
 import jax.numpy as jnp
 from jax import lax
 from jax.sharding import PartitionSpec as P
+from jax.lax import axis_index, ppermute, psum
 
 NLAG = 80
 damping = 0.1
+
+
+def _keep_up_squares(local_x, dim_k, xs):
+    part_next = local_x.shape
+    mat_out = local_x.reshape(
+        *part_next[:dim_k], xs, part_next[dim_k] // xs, *part_next[dim_k + 1 :]
+    )
+    t1 = jnp.moveaxis(mat_out, dim_k, 0)
+    return t1
+
+
+def clear_values(load, axis_k):
+    near = list(load.shape[1:])
+    near[axis_k] *= load.shape[0]
+    earlier = jnp.moveaxis(load, 0, axis_k).reshape(near)
+    return earlier
+
+
+def edit_wall(q_in, shard_axis, page, shard_in):
+    local_out, base_arr = (psum(1, shard_axis), axis_index(shard_axis))
+    val2 = _keep_up_squares(q_in, page, local_out)
+    in_order = [val2[base_arr]]
+    for ii in [*range(1, local_out)]:
+        main = val2[base_arr ^ ii]
+        in_order.append(
+            ppermute(main, shard_axis, [(tick, tick ^ ii) for tick in range(local_out)])
+        )
+    val2 = jnp.stack(in_order, axis=0)[base_arr ^ jnp.arange(local_out)]
+    ready = clear_values(val2, shard_in)
+    return ready
+
+
+answer_the_orders = functools.partial(edit_wall, shard_axis="inl", page=0, shard_in=0)
 
 
 def levinson(series):
@@ -108,13 +143,7 @@
     send_bins = jnp.take(target, source_slot, axis=0, mode="fill", fill_value=-1)
     send_rows = jnp.take(shot_rows, source_slot, axis=0, mode="fill", fill_value=0)
     arrived, arrived_bins = (
-        lax.all_to_all(
-            send_rows.reshape(devices, slots, samples),
-            "inl",
-            split_axis=0,
-            concat_axis=0,
-            tiled=True,
-        ),
+        answer_the_orders(send_rows.reshape(devices, slots, samples)),
         lax.all_to_all(
             send_bins.reshape(devices, slots), "inl", split_axis=0, concat_axis=0, tiled=True
         ),

time: 1130 us -> 1140 us (level)
  waiting for transfers between devices: 277 us -> 189 us
  starting transfers between devices: 18.1 us -> 87.6 us
  local copies, waits for them, and re-layouts: 626 us -> 655 us
    all_to_all x1 -> x0, waiting for transfers between devices: 270 us -> none  [shards(): lax.all_to_all(send_rows.reshape(devices, slots, samples), 'inl', split_a...]
    all_to_all x1, waiting for transfers between devices: 0.01 us -> 127 us  [shards(): lax.all_to_all(send_bins.reshape(devices, slots), 'inl', split_axis=0, co...]
    all_to_all x1, starting transfers between devices: 4.67 us -> 70 us  [shards(): lax.all_to_all(smoothed, 'inl', split_axis=1, concat_axis=0, tiled=True)]
    ppermute x0 -> x7, waiting for transfers between devices: none -> 54.5 us  [edit_wall(): ppermute(main, shard_axis, [(tick, tick ^ ii) for tick in range(local_out)])]
    ppermute x0 -> x7, starting transfers between devices: none -> 12.7 us  [edit_wall(): ppermute(main, shard_axis, [(tick, tick ^ ii) for tick in range(local_out)])]
    unnamed x10 -> x18, local copies, waits for them, and re-layouts: 0.02 us -> 12 us
where the time goes in v1:
time: 1140 us; the launch traced here: 1130 us
  local copies, waits for them, and re-layouts  655 us (57%)
  waiting for transfers between devices  189 us (17%)
  starting transfers between devices  87.6 us (8%)
  other arithmetic  69.3 us (6%)
  loops' own time  59.2 us (5%)
  matrix products  52.5 us (5%)
    slice x3048, local copies, waits for them, and re-layouts, autocorrelate_one_block(): within[:, offset, offset:]  406 us
    all_to_all x1, waiting for transfers between devices, shards(): lax.all_to_all(send_bins.reshape(devices, slots), 'inl', split_axis=0, co...  127 us
    slice x3048, local copies, waits for them, and re-layouts, autocorrelate_one_block(): across[:, offset, :offset]  113 us
    all_to_all x1, starting transfers between devices, shards(): lax.all_to_all(smoothed, 'inl', split_axis=1, concat_axis=0, tiled=True)  70 us
    another operation x1, loops' own time, autocorrelate(): lax.map(autocorrelate_one_block, block_rows.reshape(number // block, bloc...  59.2 us
    dynamic_update_slice x24, other arithmetic, autocorrelate(): lax.map(autocorrelate_one_block, block_rows.reshape(number // block, bloc...  55.5 us
    ppermute x7, waiting for transfers between devices, edit_wall(): ppermute(main, shard_axis, [(tick, tick ^ ii) for tick in range(local_out)])  54.5 us
    squeeze x24, local copies, waits for them, and re-layouts, autocorrelate(): lax.map(autocorrelate_one_block, block_rows.reshape(number // block, bloc...  28.3 us

profile of v1, /device:TPU:0, one launch (start us, length us, event | category | flops | bytes accessed | tf_op | source)
XLA Modules:
  0.0 1126.8 jit_solution(605811684133529745)
XLA Ops:
  3.6 2.4 scatter_custom_fusion
  7.4 9.5 gather_fusion
  16.9 24.8 %gather_fusion.1 = bf16[1536,4096]{1,0:T(8,128)(2,1)} fusion(bf16[512,4096]{1,0:T(8,128)(2,1)} %bitcast.1512, s32[2048]{0:T(1024)S(1)} %pad_clamp_fusion), kind=kCustom, calls=%fused_computation.1 | custom fusion | bytes 25171968 | tf_op jit(solution)/shard_map/jit(_take)/gather | solution.py:144
  41.7 6.3 broadcast_select_fusion
  48.1 4.6 dynamic-slice_bitcast_fusion.2
  52.7 3.0 collective-permute-start
  57.3 3.0 collective-permute-start.3
  62.2 4.9 all-to-all-start
  69.4 126.9 %all-to-all-done = s32[8,1,192]{2,1,0:T(1,128)S(1)} async-done(((s32[8,1,192]{2,1,0:T(1,128)}), s32[8,1,192]{2,1,0:T(1,128)S(1)}, u32[]{:S(2)}, u32[]{:S(2)}) %all-to-all-start) | async-done | bytes 6176 | tf_op jit(solution)/shard_map/all_to_all | solution.py:147
  196.6 3.7 collective-permute-start.5
  200.3 2.7 bitcast_dynamic-update-slice_fusion.6
  203.2 2.7 bitcast_dynamic-update-slice_fusion.5
  205.9 2.7 bitcast_dynamic-update-slice_fusion.4
  211.2 24.8 %collective-permute-done.5 = bf16[1,192,4096]{2,1,0:T(8,128)(2,1)S(1)} collective-permute-done((bf16[1,192,4096]{2,1,0:T(8,128)(2,1)}, bf16[1,192,4096]{2,1,0:T(8,128)(2,1)S(1)}, u32[]{:S(2)}, u32[]{:S(2)}) %collective-permute-start.5) | collective-permute-done | bytes 1572896 | tf_op jit(solution)/shard_map/ppermute | solution.py:36
  237.4 29.6 %collective-permute-done.6 = bf16[1,192,4096]{2,1,0:T(8,128)(2,1)S(1)} collective-permute-done((bf16[1,192,4096]{2,1,0:T(8,128)(2,1)}, bf16[1,192,4096]{2,1,0:T(8,128)(2,1)S(1)}, u32[]{:S(2)}, u32[]{:S(2)}) %collective-permute-start.6) | collective-permute-done | bytes 1572896 | tf_op jit(solution)/shard_map/ppermute | solution.py:36
  268.2 11.0 gather_fusion.2
  279.2 706.3 %while.97 = (s32[]{:T(128)}, f32[24,64,128]{2,1,0:T(8,128)S(1)}, bf16[24,64,4096]{2,1,0:T(8,128)(2,1)}, s32[]{:T(128)}) while((s32[]{:T(128)}, f32[24,64,128]{2,1,0:T(8,128)S(1)}, bf16[24,64,4096]{2,1,0:T(8,128)(2,1)}, s32[]{:T(128)}) %tuple.485), condition=%wide.region_6.7_spmd, body=%wide.region_5.6_spmd.sunk | while | flops 136298496 | bytes 32456764 | solution.py:85
  306.1 2.3 fusion.197
  335.2 2.3 fusion.197
  364.2 2.3 fusion.197
  393.3 2.3 fusion.197
  422.3 2.3 fusion.197
  451.3 2.3 fusion.197
  480.4 2.3 fusion.197
  509.4 2.3 fusion.197
  538.5 2.3 fusion.197
  567.5 2.3 fusion.197
  596.6 2.3 fusion.197
  625.6 2.3 fusion.197
  654.6 2.3 fusion.197
  683.7 2.3 fusion.197
  712.7 2.3 fusion.197
  741.8 2.3 fusion.197
  770.8 2.3 fusion.197
  799.9 2.3 fusion.197
  828.9 2.3 fusion.197
  858.0 2.3 fusion.197
  887.0 2.3 fusion.197
  916.0 2.3 fusion.197
  945.1 2.3 fusion.197
  974.1 2.3 fusion.197
  986.3 10.3 psum.7
  1024.2 6.9 fusion.124
  1031.7 2.7 fusion.129
  1034.4 4.1 fusion.130
  1040.3 70.0 %all-to-all-start.1 = ((bf16[4,16,4096]{2,0,1:T(4,128)(2,1)}), bf16[4,16,4096]{2,0,1:T(4,128)(2,1)S(1)}, u32[]{:S(2)}, u32[]{:S(2)}) async-start(bf16[4,16,4096]{2,0,1:T(4,128)(2,1)} %copy.1305), calls=%async_computation.1 | async-start | bytes 1048576 | tf_op jit(solution)/shard_map/all_to_all | solution.py:179
  1110.3 6.6 gather_fusion.4
  1117.1 8.0 all-to-all-done.1
  (6887 shorter events, 637.4 us)
Async XLA Ops:
  0.0 1110.3 %copy-start = (f32[32]{0:T(128)S(1)}, f32[32]{0:T(128)}, u32[]{:S(2)}) copy-start(f32[32]{0:T(128)} %param.175) | copy-start | bytes 388
  48.0 19.3 %copy-start.1 = (f32[16]{0:T(128)S(1)}, f32[16]{0:T(128)}, u32[]{:S(2)}) copy-start(f32[16]{0:T(128)} %param.174) | copy-start | bytes 196
  52.7 143.9 %collective-permute-start = (bf16[1,192,4096]{2,1,0:T(8,128)(2,1)}, bf16[1,192,4096]{2,1,0:T(8,128)(2,1)}, u32[]{:S(2)}, u32[]{:S(2)}) collective-permute-start(bf16[1,192,4096]{2,1,0:T(8,128)(2,1)} %get-tuple-element.1258), channel_id=1, source_target_pairs={{0,4},{4,0},{8,12},{12,8},{16,20},{20,16},{24,28},{28,24},{1,5},{5... | collective-permute-start | bytes 4718600 | tf_op jit(solution)/shard_map/ppermute | solution.py:36
  55.7 147.3 %collective-permute-start.1 = (bf16[1,192,4096]{2,1,0:T(8,128)(2,1)}, bf16[1,192,4096]{2,1,0:T(8,128)(2,1)}, u32[]{:S(2)}, u32[]{:S(2)}) collective-permute-start(bf16[1,192,4096]{2,1,0:T(8,128)(2,1)} %get-tuple-element.1257), channel_id=1, source_target_pairs={{0,8},{4,12},{8,0},{12,4},{16,24},{20,28},{24,16},{28,20},{1,9},{5... | collective-permute-start | bytes 4718600 | tf_op jit(solution)/shard_map/ppermute | solution.py:36
  57.3 148.6 %collective-permute-start.2 = (bf16[1,192,4096]{2,1,0:T(8,128)(2,1)}, bf16[1,192,4096]{2,1,0:T(8,128)(2,1)}, u32[]{:S(2)}, u32[]{:S(2)}) collective-permute-start(bf16[1,192,4096]{2,1,0:T(8,128)(2,1)} %get-tuple-element.1256), channel_id=1, source_target_pairs={{0,12},{4,8},{8,4},{12,0},{16,28},{20,24},{24,20},{28,16},{1,13},{... | collective-permute-start | bytes 4718600 | tf_op jit(solution)/shard_map/ppermute | solution.py:36
  57.3 151.4 %collective-permute-start.3 = (bf16[1,192,4096]{2,1,0:T(8,128)(2,1)}, bf16[1,192,4096]{2,1,0:T(8,128)(2,1)S(1)}, u32[]{:S(2)}, u32[]{:S(2)}) collective-permute-start(bf16[1,192,4096]{2,1,0:T(8,128)(2,1)} %get-tuple-element.1255), channel_id=1, source_target_pairs={{0,16},{4,20},{8,24},{12,28},{16,0},{20,4},{24,8},{28,12},{1,17},{... | collective-permute-start | bytes 4718600 | tf_op jit(solution)/shard_map/ppermute | solution.py:36
  60.2 149.7 %collective-permute-start.4 = (bf16[1,192,4096]{2,1,0:T(8,128)(2,1)}, bf16[1,192,4096]{2,1,0:T(8,128)(2,1)S(1)}, u32[]{:S(2)}, u32[]{:S(2)}) collective-permute-start(bf16[1,192,4096]{2,1,0:T(8,128)(2,1)} %get-tuple-element.1254), channel_id=1, source_target_pairs={{0,20},{4,16},{8,28},{12,24},{16,4},{20,0},{24,12},{28,8},{1,21},{... | collective-permute-start | bytes 4718600 | tf_op jit(solution)/shard_map/ppermute | solution.py:36
  62.2 134.1 %all-to-all-start = ((s32[8,1,192]{2,1,0:T(1,128)}), s32[8,1,192]{2,1,0:T(1,128)S(1)}, u32[]{:S(2)}, u32[]{:S(2)}) async-start(s32[8,1,192]{2,1,0:T(1,128)} %select_n.129), calls=%async_computation | async-start | bytes 16384 | tf_op jit(solution)/shard_map/all_to_all | solution.py:147
  196.6 39.5 %collective-permute-start.5 = (bf16[1,192,4096]{2,1,0:T(8,128)(2,1)}, bf16[1,192,4096]{2,1,0:T(8,128)(2,1)S(1)}, u32[]{:S(2)}, u32[]{:S(2)}) collective-permute-start(bf16[1,192,4096]{2,1,0:T(8,128)(2,1)} %get-tuple-element.1253), channel_id=1, source_target_pairs={{0,24},{4,28},{8,16},{12,20},{16,8},{20,12},{24,0},{28,4},{1,25},{... | collective-permute-start | bytes 4718600 | tf_op jit(solution)/shard_map/ppermute | solution.py:36
  203.0 64.0 %collective-permute-start.6 = (bf16[1,192,4096]{2,1,0:T(8,128)(2,1)}, bf16[1,192,4096]{2,1,0:T(8,128)(2,1)S(1)}, u32[]{:S(2)}, u32[]{:S(2)}) collective-permute-start(bf16[1,192,4096]{2,1,0:T(8,128)(2,1)} %get-tuple-element.1252), channel_id=1, source_target_pairs={{0,28},{4,24},{8,20},{12,16},{16,12},{20,8},{24,4},{28,0},{1,29},{... | collective-permute-start | bytes 4718600 | tf_op jit(solution)/shard_map/ppermute | solution.py:36
  268.2 11.0 copy-start.3
  279.2 718.5 %copy-start.2 = (f32[80,64]{1,0:T(8,128)S(1)}, f32[80,64]{1,0:T(8,128)}, u32[]{:S(2)}) copy-start(f32[80,64]{1,0:T(8,128)} %constant.2000.clone.1) | copy-start | bytes 61444
  279.2 718.5 %copy-start.4 = (f32[2,64]{1,0:T(2,128)S(1)}, f32[2,64]{1,0:T(2,128)}, u32[]{:S(2)}) copy-start(f32[2,64]{1,0:T(2,128)} %constant.2002.clone.1) | copy-start | bytes 1540
  279.2 718.5 %copy-start.5 = (f32[2,64]{1,0:T(2,128)S(1)}, f32[2,64]{1,0:T(2,128)}, u32[]{:S(2)}) copy-start(f32[2,64]{1,0:T(2,128)} %constant.2003.clone.1) | copy-start | bytes 1540
  1040.3 84.8 %all-to-all-start.1 = ((bf16[4,16,4096]{2,0,1:T(4,128)(2,1)}), bf16[4,16,4096]{2,0,1:T(4,128)(2,1)S(1)}, u32[]{:S(2)}, u32[]{:S(2)}) async-start(bf16[4,16,4096]{2,0,1:T(4,128)(2,1)} %copy.1305), calls=%async_computation.1 | async-start | bytes 1048576 | tf_op jit(solution)/shard_map/all_to_all | solution.py:179
